TPU v7x, 32 devices: a whole 2x2x4 slice. The times are simulated.
32 devices in a mesh: dp: 16 (over z, y, x), grp: 2 (over core).
Axes of the slice: x: 2, y: 2, z: 4, core: 2. Of those that a mesh axis runs over, the one named last changes fastest.
Arguments:
- audio: bfloat16 [384, 232, 320], P(('dp', 'grp')), may hold values from -3 to 3
- lengths: int32 [384], P('dp'), may hold values from 37 to 225, as said below
- codes: int32 [2, 2, 384, 232], P(None, None, 'dp'), may hold values from 0 to 1023
- disc_weight: bfloat16 [960, 512], replicated, may hold values from -0.1875 to 0.1875
- disc_score: float32 [512], replicated, may hold values from -0.25 to 0.25
- params: float32 [1441792], P('dp')
- params_mom: float32 [1441792], P('dp'), may hold values from -0.0009765625 to 0.0009765625
- params_avg: float32 [1441792], P('dp')
- books: float32 [2, 524288], P('grp', 'dp'), may hold values from -4 to 4
- books_mom: float32 [2, 524288], P('grp', 'dp'), may hold values from -3.8146973e-05 to 3.8146973e-05
- books_avg: float32 [2, 524288], P('grp', 'dp'), may hold values from -4 to 4
Outputs:
- params_new: float32 [1441792], P('dp')
- params_mom_new: float32 [1441792], P('dp')
- params_avg_new: float32 [1441792], P('dp')
- books_new: float32 [2, 524288], P('grp', 'dp')
- books_mom_new: float32 [2, 524288], P('grp', 'dp')
- books_avg_new: float32 [2, 524288], P('grp', 'dp')
- loss_sum: float32 [], replicated
- frame_count: float32 [], replicated
Inputs may be any that keep to these rules, and one draw needn't show every extreme that they name: lengths of the clips; 225 is reached in every draw.
All inputs are finite; a program needn't handle non-finite values.
Results may differ from a plain program's by a relative error of at most 0.0024.
Values may be sent and summed in bfloat16 or wider, within the bound.
A program may use at most 192 MiB of HBM per device.

v0:
```python
import math

import jax
import jax.numpy as jnp
from jax import lax
from jax.sharding import PartitionSpec as P

CB = 1024


MOMENTUM = 0.9
AVERAGE = 0.99


def spectral_table(samples):
    spots = jnp.arange(samples, dtype=jnp.int32)[:, None]
    bins = jnp.arange(samples // 2, dtype=jnp.int32)[None, :]
    turns = (spots * bins % samples).astype(jnp.float32) * (2.0 * math.pi / samples)
    window = 0.5 - 0.5 * jnp.cos((spots.astype(jnp.float32) + 0.5) * (2.0 * math.pi / samples))
    scale = math.sqrt(2.0 / samples)
    return jnp.concatenate([window * jnp.cos(turns), window * jnp.sin(turns)], axis=1) * scale


def stack_three(values):
    padded = jnp.pad(values, ((0, 0), (1, 1), (0, 0)))
    return jnp.concatenate([padded[:, :-2], padded[:, 1:-1], padded[:, 2:]], axis=2)


def unstack_three(incoming, width):
    before = incoming[..., :width]
    middle = incoming[..., width : 2 * width]
    after = incoming[..., 2 * width :]
    nothing = jnp.zeros_like(before[:, :1])
    return (
        middle
        + jnp.concatenate([before[:, 1:], nothing], 1)
        + jnp.concatenate([nothing, after[:, :-1]], 1)
    )


def project(operand, weights):
    return jnp.einsum("bsk,kd->bsd", operand, weights, preferred_element_type=jnp.float32)


def back_project(incoming, weights):
    return jnp.einsum("bsd,kd->bsk", incoming, weights, preferred_element_type=jnp.float32)


def weight_grad(operand, incoming):
    return jnp.einsum("bsk,bsd->kd", operand, incoming, preferred_element_type=jnp.float32)


def silu_slope(values):
    sigmoid = jax.nn.sigmoid(values)
    return sigmoid * (1.0 + values * (1.0 - sigmoid))


def smooth_cost(values):
    return jnp.sqrt(values * values + 1.0) - 1.0


def smooth_slope(values):
    return values / jnp.sqrt(values * values + 1.0)


def magnitude(spectrum):
    half = spectrum.shape[-1] // 2
    real_part = spectrum[..., :half]
    imag_part = spectrum[..., half:]
    return jnp.sqrt(real_part * real_part + imag_part * imag_part + 1.0)


def shards(
    audio,
    lengths,
    codes,
    disc_weight,
    disc_score,
    params,
    params_mom,
    params_avg,
    books,
    books_mom,
    books_avg,
):
    clip_count = audio.shape[0]
    slot_count = audio.shape[1]
    samples = audio.shape[2]
    width = disc_weight.shape[1]
    half_width = width // 2
    shared, table = (
        lax.all_gather(params.astype(jnp.bfloat16), "dp", axis=0, tiled=True),
        lax.all_gather(books.astype(jnp.bfloat16), "dp", axis=1, tiled=True),
    )
    enc_size = 3 * samples * width
    dec_size = 3 * width * width
    enc_weight = shared[:enc_size].reshape(3 * samples, width)
    dec_weight = shared[enc_size : enc_size + dec_size].reshape(3 * width, width)
    out_weight = shared[enc_size + dec_size :].reshape(width, samples)
    codebook = table.reshape(-1, CB, half_width)
    spec_table = spectral_table(samples).astype(jnp.bfloat16)
    side = lax.axis_index("grp")
    frames = jnp.arange(slot_count)
    pair_mask = (frames[None, :] < lengths[:, None]).astype(jnp.float32)
    own_mask = lax.dynamic_slice_in_dim(pair_mask, side * clip_count, clip_count, 0)
    local_count = jnp.sum(own_mask)
    frame_count = lax.psum(local_count, ("dp", "grp"))
    own_three = own_mask[..., None]
    pair_three = pair_mask[..., None]
    signal = audio * own_three.astype(jnp.bfloat16)
    signal_stack = stack_three(signal)
    encoded = project(signal_stack, enc_weight)
    at_group = lax.all_to_all(
        encoded.astype(jnp.bfloat16), "grp", split_axis=2, concat_axis=0, tiled=True
    )
    own_codes = lax.dynamic_index_in_dim(codes, side, 0, keepdims=False)
    entries = jnp.arange(CB)
    onehots = [
        (own_codes[level_idx][..., None] == entries).astype(jnp.bfloat16)
        for level_idx in range(own_codes.shape[0])
    ]
    picked = project(onehots[0], codebook[0])
    level_idx = 1
    picked = picked + project(onehots[level_idx], codebook[level_idx])
    code_gap = at_group.astype(jnp.float32) - picked
    commit = jnp.sum(pair_three * code_gap * code_gap) / width
    joined = lax.all_to_all(
        (picked * pair_three).astype(jnp.bfloat16), "grp", split_axis=0, concat_axis=2, tiled=True
    )
    joined_stack = stack_three(joined)
    pre_dec = project(joined_stack, dec_weight)
    hidden = jax.nn.silu(pre_dec).astype(jnp.bfloat16)
    pre_out = project(hidden, out_weight)
    tanh_out = jnp.tanh(pre_out)
    made = tanh_out * own_three
    wave_gap = made - signal.astype(jnp.float32)
    recon = jnp.sum(own_three * smooth_cost(wave_gap)) / samples
    made_low = made.astype(jnp.bfloat16)
    spec_fake = project(made_low, spec_table)
    mag_fake = magnitude(spec_fake)
    spec_gap = mag_fake - magnitude(project(signal, spec_table))
    spectral = jnp.sum(own_three * smooth_cost(spec_gap)) / samples
    pre_fake = project(stack_three(made_low), disc_weight)
    feat_fake = jax.nn.silu(pre_fake)
    feat_real = jax.nn.silu(project(signal_stack, disc_weight))
    score = jnp.sum(feat_fake * disc_score, axis=2)
    adverse = jnp.sum(own_mask * (1.0 - score) ** 2)
    feat_gap = feat_fake - feat_real
    feature = jnp.sum(own_three * smooth_cost(feat_gap)) / width
    local_loss = recon + spectral + adverse + feature + commit
    d_score = -2.0 * own_mask * (1.0 - score)
    d_feat = d_score[..., None] * disc_score + own_three * smooth_slope(feat_gap) / width
    d_pre_fake = (d_feat * silu_slope(pre_fake)).astype(jnp.bfloat16)
    d_mag = own_three * smooth_slope(spec_gap) / samples / mag_fake
    half_bins = samples // 2
    d_spec = jnp.concatenate(
        [d_mag * spec_fake[..., :half_bins], d_mag * spec_fake[..., half_bins:]], axis=2
    ).astype(jnp.bfloat16)
    d_made = unstack_three(back_project(d_pre_fake, disc_weight), samples) + back_project(
        d_spec, spec_table
    )
    d_made = d_made + own_three * smooth_slope(wave_gap) / samples
    d_pre_out = (d_made * own_three * (1.0 - tanh_out * tanh_out)).astype(jnp.bfloat16)
    grad_out = weight_grad(hidden, d_pre_out)
    d_pre_dec = (back_project(d_pre_out, out_weight) * silu_slope(pre_dec)).astype(jnp.bfloat16)
    grad_dec = weight_grad(joined_stack, d_pre_dec)
    d_joined = unstack_three(back_project(d_pre_dec, dec_weight), width).astype(jnp.bfloat16)
    d_quant = lax.all_to_all(d_joined, "grp", split_axis=2, concat_axis=0, tiled=True)
    commit_slope = 2.0 * pair_three * code_gap / width
    d_picked = (-commit_slope).astype(jnp.bfloat16)
    grad_book = jnp.stack(
        [weight_grad(onehot_table, d_picked) for onehot_table in onehots]
    ).reshape(1, -1)
    d_latent = (d_quant.astype(jnp.float32) * pair_three + commit_slope).astype(jnp.bfloat16)
    d_encoded = lax.all_to_all(d_latent, "grp", split_axis=0, concat_axis=2, tiled=True)
    grad_enc = weight_grad(signal_stack, d_encoded)
    grad_shared = jnp.concatenate(
        [grad_enc.reshape(-1), grad_dec.reshape(-1), grad_out.reshape(-1)]
    )
    grad_shared = lax.psum(grad_shared.astype(jnp.bfloat16), "grp").astype(jnp.float32)
    shared_part, book_part = (
        lax.psum_scatter(grad_shared, "dp", scatter_dimension=0, tiled=True),
        lax.psum_scatter(grad_book, "dp", scatter_dimension=1, tiled=True),
    )
    loss_sum = lax.psum(local_loss, ("dp", "grp"))
    all_clips = clip_count * lax.axis_size("dp") * lax.axis_size("grp")
    root = math.sqrt(131.0 * all_clips)
    shard_length = params.shape[0]
    spots = lax.axis_index("dp") * shard_length + jnp.arange(shard_length)
    rate = (
        jnp.where(spots < enc_size, 0.65, jnp.where(spots < enc_size + dec_size, 0.14, 0.2)) * root
    )
    shared_grad = shared_part / frame_count
    mom_new = MOMENTUM * params_mom + shared_grad
    param_new = params - rate * (shared_grad + MOMENTUM * mom_new)
    avg_new = AVERAGE * params_avg + (1.0 - AVERAGE) * param_new
    book_rate = 3.9 * math.sqrt(131.0 * all_clips * CB)
    book_grad = book_part / frame_count
    book_mom_new = MOMENTUM * books_mom + book_grad
    book_new = books - book_rate * (book_grad + MOMENTUM * book_mom_new)
    book_avg_new = AVERAGE * books_avg + (1.0 - AVERAGE) * book_new
    return (
        param_new,
        mom_new,
        avg_new,
        book_new,
        book_mom_new,
        book_avg_new,
        loss_sum,
        frame_count,
    )


def solution(mesh):
    in_specs = (
        P(("dp", "grp"), None, None),
        P("dp"),
        P(None, None, "dp", None),
        P(),
        P(),
        P("dp"),
        P("dp"),
        P("dp"),
        P("grp", "dp"),
        P("grp", "dp"),
        P("grp", "dp"),
    )
    out_specs = (
        P("dp"),
        P("dp"),
        P("dp"),
        P("grp", "dp"),
        P("grp", "dp"),
        P("grp", "dp"),
        P(),
        P(),
    )
    return jax.shard_map(shards, mesh=mesh, in_specs=in_specs, out_specs=out_specs, check_vma=False)
```

profile of v0, /device:TPU:0, one launch (start us, length us, event | category | flops | bytes accessed | tf_op | source)
XLA Modules:
  0.0 766.0 jit_solution(17068021290034561460)
XLA Ops:
  17.3 57.5 %all-gather.3.cloned.1.call-done = bf16[1,524288]{1,0:T(2,128)(2,1)} async-done(((bf16[1,32768]{1,0:T(2,128)(2,1)}), bf16[1,524288]{1,0:T(2,128)(2,1)}) %all-gather.3.cloned.1.call-update) | async-done | bytes 1048592 | tf_op jit(solution)/shard_map/all_gather | solution.py:93
  74.8 12.3 %slice_reduce_fusion = (bf16[262144]{0:T(1024)(128)(2,1)S(1)}, bf16[262144]{0:T(1024)(128)(2,1)S(1)}) fusion(bf16[1,524288]{1,0:T(2,128)(2,1)} %all-gather.3.cloned.1.call-done), kind=kLoop, calls=%fused_computation.87 | loop fusion | bytes 2097152 | tf_op jit(solution)/shard_map/slice | solution.py:124
  87.5 5.1 fusion.1
  92.6 7.3 multiply_convert_fusion.3
  99.9 6.2 all_to_all.54
  111.1 31.6 %all-gather.5.cloned.1.call-done = bf16[1441792]{0:T(1024)(128)(2,1)} async-done(((bf16[90112]{0:T(1024)(128)(2,1)}), bf16[1441792]{0:T(1024)(128)(2,1)}) %all-gather.5.cloned.1.call-update) | async-done | bytes 2883600 | tf_op jit(solution)/shard_map/all_gather | solution.py:92
  147.4 9.9 %multiply_convert_fusion.2 = (bf16[12,232,512]{2,1,0:T(8,128)(2,1)S(1)}, f32[12,232,512]{2,1,0:T(8,128)}) fusion(bf16[1536,512,1]{1,0,2:T(8,128)(2,1)} %reshape.142, bf16[12,232,512]{2,1,0:T(8,128)(2,1)} %get-tuple-element.37, bf16[12,232,512]{2,1,0:T(8,128)(2,1)} %bitcast.100, bf16[12,232,512]{2,1,0:T(8,128)(2,1)} %get-tuple-element.36), kind=kOutput, calls=%fused_computation.37 | convolution fusion | flops 4411637760 | bytes 18677760 | tf_op jit(solution)/shard_map/bsk,kd->bsd/dot_general | solution.py:42
  157.4 6.0 multiply_reduce_fusion.2
  172.3 10.6 %multiply_reduce_fusion = (f32[]{:T(128)}, f32[12,232]{1,0:T(8,128)S(1)}, f32[12,232,512]{2,1,0:T(8,128)}) fusion(f32[12,232]{1,0:T(8,128)S(1)} %get-tuple-element.30, f32[12,232,512]{2,1,0:T(8,128)S(1)} %fusion.8, f32[512]{0:T(512)S(1)} %copy-done.31, bf16[960,512]{1,0:T(8,128)(2,1)S(1)} %copy-done, bf16[12,232,320]{1,2,0:T(8,128)(2,1)S(1)} %get-tuple-element.41, ...), kind=kOutput, calls=%fused_computation.27 | convolution fusion | flops 2775622912 | bytes 17755908 | tf_op jit(solution)/shard_map/bsk,kd->bsd/dot_general | solution.py:42
  183.5 11.9 %fusion.30 = f32[12,232,960]{1,2,0:T(8,128)S(1)} fusion(f32[12,232,512]{2,1,0:T(8,128)} %copy-done.34, f32[12,232,512]{2,1,0:T(8,128)} %get-tuple-element.52, f32[12,232]{1,0:T(8,128)S(1)} %get-tuple-element.30, f32[12,232]{1,0:T(8,128)S(1)} %get-tuple-element.44, f32[512]{0:T(512)S(1)} %copy-done.31, bf16[960,512]{1,0:T(8,128)(2,1)S(1)} %copy-done), kind=kOutput, calls=%fused_computation.56 | convolution fusion | flops 2768142336 | bytes 23101184 | tf_op jit(solution)/shard_map/bsd,kd->bsk/dot_general | solution.py:46
  204.9 7.2 fusion.25
  213.3 4.8 multiply_convert_fusion
  218.1 8.5 %fusion.79 = f32[12,232,1536]{2,1,0:T(8,128)} fusion(bf16[12,232,512]{2,1,0:T(8,128)(2,1)S(1)} %multiply_convert_fusion, bf16[1536,512,1]{1,0,2:T(8,128)(2,1)S(1)} %copy-done.13), kind=kOutput, calls=%fused_computation.142 | convolution fusion | flops 4378853376 | bytes 21528576 | tf_op jit(solution)/shard_map/bsd,kd->bsk/dot_general | solution.py:46
  226.6 5.9 fusion.38
  232.5 8.2 %fusion.77 = (f32[12,231,512]{2,1,0:T(8,128)S(1)}, f32[12,231,512]{2,1,0:T(8,128)}) fusion(f32[12,232,1536]{2,1,0:T(8,128)} %fusion.79), kind=kLoop, calls=%fused_computation.140 | loop fusion | bytes 22708224 | tf_op jit(solution)/shard_map/slice | solution.py:36
  240.6 8.2 %fusion.16 = bf16[12,232,512]{2,1,0:T(8,128)(2,1)} fusion(f32[12,232,1536]{2,1,0:T(8,128)} %fusion.79, f32[12,231,512]{2,1,0:T(8,128)} %get-tuple-element.32, f32[12,231,512]{2,1,0:T(8,128)S(1)} %get-tuple-element.31), kind=kLoop, calls=%fused_computation.22 | loop fusion | flops 4276224 | bytes 19906560 | tf_op jit(solution)/shard_map/convert_element_type | solution.py:167
  248.8 7.8 %copy.55 = bf16[12,232,512]{1,0,2:T(8,128)(2,1)} copy(bf16[12,232,512]{2,1,0:T(8,128)(2,1)} %fusion.16) | data formatting | bytes 5701632 | tf_op jit(solution)/shard_map/convert_element_type | solution.py:167
  256.6 11.8 %all_to_all.55 = bf16[12,232,512]{1,0,2:T(8,128)(2,1)} all-to-all(bf16[12,232,512]{1,0,2:T(8,128)(2,1)} %copy.55), channel_id=1, replica_groups=mesh['dp'=16,'grp'=2] {'grp'}, dimensions={2} | all-to-all | bytes 5701632 | tf_op jit(solution)/shard_map/all_to_all | solution.py:168
  268.5 8.3 %copy.56 = f32[12,232,2,256]{3,1,0,2:T(8,128)} copy(bf16[12,232,2,256]{1,0,3,2:T(8,128)(2,1)} %bitcast.97) | data formatting | bytes 8552448 | tf_op jit(solution)/shard_map/convert_element_type | solution.py:174
  278.3 7.1 convolution_convert_fusion
  285.4 7.8 %copy.58 = bf16[12,232,512]{1,0,2:T(8,128)(2,1)} copy(bf16[12,232,512]{2,1,0:T(8,128)(2,1)} %convolution_convert_fusion) | data formatting | bytes 5701632 | tf_op jit(solution)/shard_map/convert_element_type | solution.py:114
  293.2 11.8 %all_to_all.56 = bf16[12,232,512]{1,0,2:T(8,128)(2,1)} all-to-all(bf16[12,232,512]{1,0,2:T(8,128)(2,1)} %copy.58), channel_id=1, replica_groups=mesh['dp'=16,'grp'=2] {'grp'}, dimensions={2} | all-to-all | bytes 5701632 | tf_op jit(solution)/shard_map/all_to_all | solution.py:113
  305.1 8.1 %copy.59 = f32[12,232,2,256]{3,1,0,2:T(8,128)} copy(bf16[12,232,2,256]{1,0,3,2:T(8,128)(2,1)} %bitcast.98) | data formatting | bytes 8552448 | tf_op jit(solution)/shard_map/convert_element_type | solution.py:125
  313.2 10.3 %fusion.18 = (bf16[24,232,256]{2,1,0:T(8,128)(2,1)}, f32[24,232,256]{2,1,0:T(8,128)S(1)}) fusion(f32[12,232,2,256]{3,1,0,2:T(8,128)} %copy.56, f32[24,232]{1,0:T(8,128)S(1)} %copy-done.25, f32[24,232]{1,0:T(8,128)S(1)} %copy-done.22, f32[24,232,256]{2,1,0:T(8,128)} %get-tuple-element.48, f32[24,232,256]{2,1,0:T(8,128)} %copy-done.5, f32[12,232,2,256]{3,1,0,2:T(8,128)} %copy.59), kind=kLoop, calls=%fused_computation.26 | loop fusion | flops 9977856 | bytes 31403520 | tf_op jit(solution)/shard_map/convert_element_type | solution.py:174
  323.5 8.9 %fusion.40 = f32[1,1024,256]{2,1,0:T(8,128)} fusion(s32[24,232]{1,0:T(8,128)S(1)} %copy-done.29, f32[24,232,256]{2,1,0:T(8,128)S(1)} %get-tuple-element.23, f32[24,232]{1,0:T(8,128)S(1)} %copy-done.25), kind=kOutput, calls=%fused_computation.83 | convolution fusion | flops 2930638848 | bytes 6794752 | tf_op jit(solution)/shard_map/bsk,bsd->kd/dot_general | solution.py:50
  332.4 9.1 %fusion.39 = f32[1,1024,256]{2,1,0:T(8,128)} fusion(s32[24,232]{1,0:T(8,128)S(1)} %copy-done.27, f32[24,232,256]{2,1,0:T(8,128)S(1)} %get-tuple-element.23, f32[24,232]{1,0:T(8,128)S(1)} %copy-done.25), kind=kOutput, calls=%fused_computation.82 | convolution fusion | flops 2930638848 | bytes 6794752 | tf_op jit(solution)/shard_map/bsk,bsd->kd/dot_general | solution.py:50
  345.5 7.3 all_to_all.57
  362.1 11.9 %pad_maximum_fusion.8 = bf16[1441792]{0:T(1024)(128)(2,1)} fusion(bf16[163840]{0:T(1024)(128)(2,1)S(1)} %reshape.134, bf16[786432]{0:T(1024)(128)(2,1)} %bitcast.104, bf16[491520]{0:T(1024)(128)(2,1)S(1)} %bitcast.105), kind=kLoop, calls=%fused_computation.55 | loop fusion | flops 8650752 | bytes 5767168 | tf_op jit(solution)/shard_map/concatenate | solution.py:177
  381.5 40.5 %all-reduce.9 = (f32[]{:T(128)}, f32[]{:T(128)}) all-reduce(f32[]{:T(128)} %get-tuple-element.13, f32[]{:T(128)S(6)} %add.193), channel_id=1, replica_groups=mesh['dp'=16,'grp'=2] {'dp','grp'}, use_global_device_ids=true, to_apply=%region_4.5 | all-reduce | flops 2 | bytes 16 | tf_op jit(solution)/shard_map/psum | solution.py:107
  422.0 65.4 %all-reduce.16.cloned.1.call-done = f32[1,524288]{1,0:T(1,128)} async-done(((f32[1,524288]{1,0:T(1,128)}), f32[1,524288]{1,0:T(1,128)}) %all-reduce.16.cloned.1.call-update) | async-done | bytes 2097168
  490.3 21.4 %all-reduce.14.cloned.1.call-done = bf16[1441792]{0:T(1024)(128)(2,1)} async-done(((bf16[1441792]{0:T(1024)(128)(2,1)}), bf16[1441792]{0:T(1024)(128)(2,1)}) %all-reduce.14.cloned.1.call-update) | async-done | bytes 2883600 | tf_op jit(solution)/shard_map/psum | solution.py:180
  511.7 244.5 %all-reduce.17 = f32[1441792]{0:T(1024)} all-reduce(bf16[1441792]{0:T(1024)(128)(2,1)} %all-reduce.14.cloned.1.call-done), channel_id=2, replica_groups=mesh['dp'=16,'grp'=2] {'dp'}, use_global_device_ids=true, to_apply=%region_2.3.clone | all-reduce | flops 1441792 | bytes 8650752
  (121 shorter events, 63.6 us)
Async XLA Ops:
  7.2 161.8 %copy-start = (bf16[960,512]{1,0:T(8,128)(2,1)S(1)}, bf16[960,512]{1,0:T(8,128)(2,1)}, u32[]{:S(2)}) copy-start(bf16[960,512]{1,0:T(8,128)(2,1)} %param.14) | copy-start | bytes 2949124
  7.2 67.6 %all-gather.3.cloned.1.call-start = ((), (), s32[]{:S(2)}) async-start(), calls=%async_computation.4 | async-start | bytes 2228224 | tf_op jit(solution)/shard_map/all_gather | solution.py:93
  9.0 133.7 %all-gather.5.cloned.1.call-start = ((), (), s32[]{:S(2)}) async-start(), calls=%async_computation.5 | async-start | bytes 3063808 | tf_op jit(solution)/shard_map/all_gather | solution.py:92
  10.7 476.6 %all-reduce.16.cloned.1.call-start = ((), (), s32[]{:S(2)}) async-start(), calls=%async_computation.7 | async-start | bytes 4194304
  14.1 78.5 %copy-start.21 = (f32[24,232]{1,0:T(8,128)}, f32[24,232]{1,0:T(8,128)S(1)}, u32[]{:S(2)}) copy-start(f32[24,232]{1,0:T(8,128)S(1)} %fusion.60) | copy-start | bytes 66820
  14.9 77.7 %copy-start.28 = (s32[24,232]{1,0:T(8,128)}, s32[24,232]{1,0:T(8,128)S(1)}, u32[]{:S(2)}) copy-start(s32[24,232]{1,0:T(8,128)S(1)} %get-tuple-element.42) | copy-start | bytes 66820
  14.9 77.7 %copy-start.26 = (s32[24,232]{1,0:T(8,128)}, s32[24,232]{1,0:T(8,128)S(1)}, u32[]{:S(2)}) copy-start(s32[24,232]{1,0:T(8,128)S(1)} %get-tuple-element.43) | copy-start | bytes 66820
  92.6 7.4 copy-start.5
  147.4 9.9 %copy-start.18 = (bf16[512,320]{1,0:T(8,128)(2,1)S(1)}, bf16[512,320]{1,0:T(8,128)(2,1)}, u32[]{:S(2)}) copy-start(bf16[512,320]{1,0:T(8,128)(2,1)} %reshape.131) | copy-start | bytes 983044
  147.4 9.9 %copy-start.30 = (bf16[12,232,320]{1,2,0:T(8,128)(2,1)S(1)}, bf16[12,232,320]{1,2,0:T(8,128)(2,1)}, u32[]{:S(2)}) copy-start(bf16[12,232,320]{1,2,0:T(8,128)(2,1)} %param.11) | copy-start | bytes 5345284
  157.4 6.0 copy-start.32
  166.5 5.8 copy-start.9
  166.5 5.8 copy-start.11
  172.3 10.6 %copy-start.34 = (f32[12,232,512]{2,1,0:T(8,128)}, f32[12,232,512]{2,1,0:T(8,128)S(1)}, u32[]{:S(2)}) copy-start(f32[12,232,512]{2,1,0:T(8,128)S(1)} %fusion.8) | copy-start | bytes 17104900
  204.9 7.2 copy-start.33
  218.1 8.5 %copy-start.4 = (bf16[2,12,29,8,256]{4,3,0,2,1:T(8,128)(2,1)S(1)}, bf16[2,12,29,8,256]{4,3,0,2,1:T(8,128)(2,1)}, u32[]{:S(2)}) copy-start(bf16[2,12,29,8,256]{4,3,0,2,1:T(8,128)(2,1)} %copy-done.3) | copy-start | bytes 8552452
  218.1 8.5 %copy-start.7 = (bf16[12,232,512]{2,1,0:T(8,128)(2,1)S(1)}, bf16[12,232,512]{2,1,0:T(8,128)(2,1)}, u32[]{:S(2)}) copy-start(bf16[12,232,512]{2,1,0:T(8,128)(2,1)} %get-tuple-element.36) | copy-start | bytes 8552452
  218.1 8.5 %copy-start.8 = (bf16[12,232,512]{2,1,0:T(8,128)(2,1)S(1)}, bf16[12,232,512]{2,1,0:T(8,128)(2,1)}, u32[]{:S(2)}) copy-start(bf16[12,232,512]{2,1,0:T(8,128)(2,1)} %get-tuple-element.37) | copy-start | bytes 8552452
  268.5 8.3 %slice-start.2 = ((bf16[1441792]{0:T(1024)(128)(2,1)}), bf16[491520]{0:T(1024)(128)(2,1)S(1)}, s32[]{:S(2)}) async-start(bf16[1441792]{0:T(1024)(128)(2,1)} %all-gather.5.cloned.1.call-done), calls=%async_computation.10 | async-start | bytes 1966080 | tf_op jit(solution)/shard_map/slice | solution.py:97
  305.1 8.1 %copy-start.22 = (f32[24,232]{1,0:T(8,128)S(1)}, f32[24,232]{1,0:T(8,128)}, u32[]{:S(2)}) copy-start(f32[24,232]{1,0:T(8,128)} %copy-done.21) | copy-start | bytes 66820
  305.1 8.1 %copy-start.25 = (f32[24,232]{1,0:T(8,128)S(1)}, f32[24,232]{1,0:T(8,128)}, u32[]{:S(2)}) copy-start(f32[24,232]{1,0:T(8,128)} %fusion.59) | copy-start | bytes 66820
  313.2 10.3 %copy-start.29 = (s32[24,232]{1,0:T(8,128)S(1)}, s32[24,232]{1,0:T(8,128)}, u32[]{:S(2)}) copy-start(s32[24,232]{1,0:T(8,128)} %copy-done.28) | copy-start | bytes 66820
  323.5 8.9 %copy-start.2 = (f32[24,232,256]{2,1,0:T(8,128)}, f32[24,232,256]{2,1,0:T(8,128)S(1)}, u32[]{:S(2)}) copy-start(f32[24,232,256]{2,1,0:T(8,128)S(1)} %get-tuple-element.23) | copy-start | bytes 17104900
  323.5 8.9 %copy-start.27 = (s32[24,232]{1,0:T(8,128)S(1)}, s32[24,232]{1,0:T(8,128)}, u32[]{:S(2)}) copy-start(s32[24,232]{1,0:T(8,128)} %copy-done.26) | copy-start | bytes 66820
  362.0 149.7 %all-reduce.14.cloned.1.call-start = ((), (), s32[]{:S(2)}) async-start(), calls=%async_computation.6 | async-start | bytes 5767168 | tf_op jit(solution)/shard_map/psum | solution.py:180
  374.6 112.7 %copy-start.17 = (f32[1,32768]{1,0:T(1,128)S(1)}, f32[1,32768]{1,0:T(1,128)}, u32[]{:S(2)}) copy-start(f32[1,32768]{1,0:T(1,128)} %param.19) | copy-start | bytes 393220
  374.6 112.7 %copy-start.23 = (f32[1,32768]{1,0:T(1,128)S(1)}, f32[1,32768]{1,0:T(1,128)}, u32[]{:S(2)}) copy-start(f32[1,32768]{1,0:T(1,128)} %param.21) | copy-start | bytes 393220
  374.6 112.7 %copy-start.24 = (f32[1,32768]{1,0:T(1,128)S(1)}, f32[1,32768]{1,0:T(1,128)}, u32[]{:S(2)}) copy-start(f32[1,32768]{1,0:T(1,128)} %param.20) | copy-start | bytes 393220
  487.3 271.7 %copy-start.1 = (bf16[960,512]{1,0:T(8,128)(2,1)S(1)}, bf16[960,512]{1,0:T(8,128)(2,1)}, u32[]{:S(2)}) copy-start(bf16[960,512]{1,0:T(8,128)(2,1)} %param.14) | copy-start | bytes 2949124
  490.3 266.0 %copy-start.14 = (f32[90112]{0:T(1024)S(1)}, f32[90112]{0:T(1024)}, u32[]{:S(2)}) copy-start(f32[90112]{0:T(1024)} %param.16) | copy-start | bytes 1081348
  490.3 266.0 %copy-start.19 = (f32[90112]{0:T(1024)S(1)}, f32[90112]{0:T(1024)}, u32[]{:S(2)}) copy-start(f32[90112]{0:T(1024)} %param.18) | copy-start | bytes 1081348
  490.3 266.0 %copy-start.20 = (f32[90112]{0:T(1024)S(1)}, f32[90112]{0:T(1024)}, u32[]{:S(2)}) copy-start(f32[90112]{0:T(1024)} %param.17) | copy-start | bytes 1081348
  (10 other events, 27.4 us)
Sparse Core Ops, SparseCore 0:
  11.4 63.3 all-gather.2
  78.1 64.5 all-gather.4
  362.1 125.1 all-reduce.15
  489.6 22.0 all-reduce.13
where the time goes:
time: 775 us; the launch traced here: 766 us
  blocking collectives  322 us (42%)
  waiting for transfers between devices  176 us (23%)
  matrix products  112 us (14%)
  local copies, waits for them, and re-layouts  84.2 us (11%)
  other arithmetic  52.2 us (7%)
  between operations  19.2 us (2%)
    unnamed x1, blocking collectives  245 us
    unnamed x5, waiting for transfers between devices  65.4 us
    all_gather x1, waiting for transfers between devices, shards(): lax.all_gather(books.astype(jnp.bfloat16), 'dp', axis=1, tiled=True)  57.5 us
    dot_general x9, matrix products, project(): jnp.einsum('bsk,kd->bsd', operand, weights, preferred_element_type=jnp.fl...  51.7 us
    psum x1, blocking collectives, shards(): frame_count = lax.psum(local_count, ('dp', 'grp'))  40.5 us
    dot_general x4, matrix products, back_project(): jnp.einsum('bsd,kd->bsk', incoming, weights, preferred_element_type=jnp.f...  32.4 us
    all_gather x1, waiting for transfers between devices, shards(): lax.all_gather(params.astype(jnp.bfloat16), 'dp', axis=0, tiled=True)  31.6 us
    dot_general x5, matrix products, weight_grad(): jnp.einsum('bsk,bsd->kd', operand, incoming, preferred_element_type=jnp.f...  28 us
  transfers between devices with their start and end apart: 4, of which 4 were waited for; matrix products, arithmetic and copies ran while one was open for 7% of the time, Pallas kernels for 0%

commit v1 on v0

v1 whole, which is shorter than its diff:
```python
import math

import jax
import jax.numpy as jnp
import numpy as np
from jax import lax
from jax.experimental import pallas as pl
from jax.experimental.pallas import tpu as pltpu
from jax.sharding import PartitionSpec as P

BF = jnp.bfloat16
F32 = jnp.float32
MOMENTUM = 0.9
AVERAGE = 0.99
LANES = 256
CB = 1024
WIDE = 512


def spectral_table(samples):
    spots = np.arange(samples)[:, None]
    bins = np.arange(samples // 2)[None, :]
    turns = (spots * bins % samples) * (2.0 * math.pi / samples)
    window = 0.5 - 0.5 * np.cos((spots + 0.5) * (2.0 * math.pi / samples))
    table = np.concatenate([window * np.cos(turns), window * np.sin(turns)], axis=1)
    return (table * math.sqrt(2.0 / samples)).astype(np.float32)


def dot(left, right):
    return jnp.dot(left, right, preferred_element_type=F32)


def dot_nt(left, right):
    return lax.dot_general(left, right, (((1,), (1,)), ((), ())), preferred_element_type=F32)


def lanes(index, width):
    return pl.ds(pl.multiple_of(index * width, width), width)


def col_sum(values):
    return jnp.sum(values, axis=0, keepdims=True)


def before(values):
    return pltpu.roll(values, 1, 1)


def after(values):
    return pltpu.roll(values, values.shape[1] - 1, 1)


def stack_three(values):
    return jnp.concatenate([before(values), values, after(values)], axis=0)


def silu_parts(values):
    sigmoid = 0.5 * jnp.tanh(0.5 * values) + 0.5
    return values * sigmoid, sigmoid * (1.0 + values * (1.0 - sigmoid))


def silu(values):
    return values * (0.5 * jnp.tanh(0.5 * values) + 0.5)


def load_signal(clip_count, side, aud, lens, codes, pad, ipad, crow, mask, sig):
    slots = aud.shape[2]
    samples = aud.shape[1]
    pad[...] = jnp.zeros_like(pad)
    ipad[...] = jnp.full(ipad.shape, -1, jnp.int32)
    spots = lax.broadcasted_iota(jnp.int32, (1, LANES), 1)

    def step(clip, carry):
        here = lanes(clip, LANES)
        row = side * clip_count + clip
        own = (spots < lens[row]).astype(F32)
        mask[:, here] = own
        for which in range(4):
            ipad[which : which + 1, 0:slots] = codes[which // 2, which % 2, pl.ds(row, 1), :]
        crow[:, here] = ipad[...]
        pad[:, 0:slots] = aud[clip]
        wave = pad[...].astype(F32) * own
        sig[:, here] = wave.astype(BF)
        return carry

    lax.fori_loop(0, clip_count, step, 0)


def real_side(clip_count, sig, disc_t, spec_t, feat_real, mag_real):
    samples = spec_t.shape[0]
    half = samples // 2

    def step(pair, carry):
        here = lanes(pair, WIDE)
        wave = sig[:, here]
        feat_real[:, here] = silu(dot(disc_t[...], stack_three(wave))).astype(BF)
        spec = dot(spec_t[...], wave)
        norm = spec[:half] * spec[:half] + spec[half:] * spec[half:] + 1.0
        mag_real[:, here] = jnp.sqrt(norm)
        return carry

    lax.fori_loop(0, clip_count * LANES // WIDE, step, 0)


def onehot(crow, which, here, count):
    entries = lax.broadcasted_iota(jnp.int32, (CB, count), 0)
    return (entries == crow[pl.ds(which, 1), here]).astype(F32).astype(BF)


def pick(clip_count, crow, mask, books_t, quant, low):
    half = books_t.shape[1]

    def step(pair, carry):
        here = lanes(pair, WIDE)
        own = mask[:, here]
        for group in range(2):
            hot = jnp.concatenate(
                [onehot(crow, 2 * group, here, WIDE), onehot(crow, 2 * group + 1, here, WIDE)], 0
            )
            value = dot(books_t[group], hot) * own
            high = value.astype(BF)
            spot = group * half
            low[spot : spot + half, here] = (value - high.astype(F32)).astype(BF)
            quant[spot : spot + half, here] = high
        return carry

    lax.fori_loop(0, clip_count * LANES // WIDE, step, 0)


def encode(clip_count, enc_t, sig, quant, low, mask, slope, loss):
    width = enc_t.shape[0]

    def step(pair, carry):
        here = lanes(pair, WIDE)
        latent = dot(enc_t[...], stack_three(sig[:, here])).astype(BF).astype(F32)
        value = quant[:, here].astype(F32) + low[:, here].astype(F32)
        gap = (latent - value) * mask[:, here]
        loss[...] += col_sum(gap * gap) * (1.0 / width)
        slope[:, here] = (gap * (-2.0 / width)).astype(BF)
        return carry

    lax.fori_loop(0, clip_count * LANES // WIDE, step, 0)


def book_grad(clip_count, crow, slope, which, group_rows):
    total = None
    chunk = 4 * LANES
    for part in range(clip_count * LANES // chunk):
        here = pl.ds(part * chunk, chunk)
        term = dot_nt(onehot(crow, which, here, chunk), slope[group_rows, here])
        total = term if total is None else total + term
    return total


def decode(clip_count, refs, loss):
    (quant, dec_t, out, out_t, mask, sig, spec, spec_t, disc, disc_t, score_col) = refs[:11]
    (feat_real, mag_real, hidden, d_out, d_dec) = refs[11:]
    samples = spec.shape[0]
    width = hidden.shape[0]
    half = samples // 2

    def step(pair, carry):
        here = lanes(pair, WIDE)
        own = mask[:, here]
        pre_dec = dot(dec_t[...], stack_three(quant[:, here]))
        act, act_slope = silu_parts(pre_dec)
        act = act.astype(BF)
        hidden[:, here] = act
        tanh_out = jnp.tanh(dot(out_t[...], act))
        made = tanh_out * own
        wave_gap = made - sig[:, here].astype(F32)
        norm = wave_gap * wave_gap + 1.0
        root = lax.rsqrt(norm)
        lost = col_sum(norm * root - 1.0) * (1.0 / samples)
        d_made = wave_gap * root * (1.0 / samples)
        made_low = made.astype(BF)

        spec_fake = dot(spec_t[...], made_low)
        real_part, imag_part = spec_fake[:half], spec_fake[half:]
        norm = real_part * real_part + imag_part * imag_part + 1.0
        root = lax.rsqrt(norm)
        spec_gap = norm * root - mag_real[:, here]
        norm = spec_gap * spec_gap + 1.0
        gap_root = lax.rsqrt(norm)
        lost += col_sum(norm * gap_root - 1.0) * (1.0 / samples)
        d_mag = spec_gap * gap_root * root * (1.0 / samples)
        d_spec = jnp.concatenate([d_mag * real_part, d_mag * imag_part], axis=0).astype(BF)
        d_made += dot(spec[...], d_spec)

        pre_fake = dot(disc_t[...], stack_three(made_low))
        feat_fake, feat_slope = silu_parts(pre_fake)
        weight = jnp.concatenate([score_col[...]] * (WIDE // 128), axis=1)
        miss = 1.0 - col_sum(feat_fake * weight)
        feat_gap = feat_fake - feat_real[:, here].astype(F32)
        norm = feat_gap * feat_gap + 1.0
        root = lax.rsqrt(norm)
        lost += own * (miss * miss + col_sum(norm * root - 1.0) * (1.0 / width))
        d_feat = (-2.0 * own * miss) * weight + (own * (1.0 / width)) * (feat_gap * root)
        d_fake = (d_feat * feat_slope).astype(BF)
        back = dot(disc[...], d_fake)
        d_made += after(back[:samples]) + back[samples : 2 * samples] + before(back[2 * samples :])

        d_pre_out = (d_made * own * (1.0 - tanh_out * tanh_out)).astype(BF)
        d_out[:, here] = d_pre_out
        d_dec[:, here] = (dot(out[...], d_pre_out) * act_slope).astype(BF)
        loss[...] += lost
        return carry

    lax.fori_loop(0, clip_count * LANES // WIDE, step, 0)


def latent_back(clip_count, dec, d_dec, mask, slope, d_latent):
    width = d_dec.shape[0]

    def step(pair, carry):
        here = lanes(pair, WIDE)
        back = dot(dec[...], d_dec[:, here])
        joined = after(back[:width]) + back[width : 2 * width] + before(back[2 * width :])
        joined = joined.astype(BF).astype(F32) * mask[:, here]
        d_latent[:, here] = (joined - slope[:, here].astype(F32)).astype(BF)
        return carry

    lax.fori_loop(0, clip_count * LANES // WIDE, step, 0)


def local_kernel(
    aud, lens, codes, disc, score, spec, spec_t, enc, dec, out, books,
    g_enc, g_dec, g_out, g_books, loss_out,
    pad, ipad, crow, mask, sig, disc_t, score_col, feat_real, mag_real,
    books_t, quant, hidden, enc_t, slope, dec_t, out_t, d_out, d_dec, loss,
    met, send_sem, recv_sem,
):
    clip_count = aud.shape[0]
    side = lax.axis_index("grp")
    spot = lax.axis_index("dp")
    barrier = pltpu.get_barrier_semaphore()
    pl.semaphore_signal(
        barrier, inc=1, device_id=(spot, 1 - side), device_id_type=pl.DeviceIdType.MESH
    )
    pl.semaphore_wait(barrier, 1)
    loss[...] = jnp.zeros_like(loss)
    disc_t[...] = jnp.transpose(disc[...])
    score_col[...] = jnp.transpose(jnp.broadcast_to(score[...], (128, score.shape[1])))
    load_signal(clip_count, side, aud, lens, codes, pad, ipad, crow, mask, sig)
    real_side(clip_count, sig, disc_t, spec_t, feat_real, mag_real)
    for group in range(2):
        books_t[group] = jnp.transpose(books[group])
    pick(clip_count, crow, mask, books_t, quant, hidden)
    enc_t[...] = jnp.transpose(enc[...])
    dec_t[...] = jnp.transpose(dec[...])
    out_t[...] = jnp.transpose(out[...])
    encode(clip_count, enc_t, sig, quant, hidden, mask, slope, loss)

    def book_step(which, carry):
        rows = pl.ds(pl.multiple_of(which // 2 * 256, 256), 256)
        g_books[which] = book_grad(clip_count, crow, slope, which, rows)
        return carry

    lax.fori_loop(0, 4, book_step, 0)
    decode(
        clip_count,
        (quant, dec_t, out, out_t, mask, sig, spec, spec_t, disc, disc_t, score_col,
         feat_real, mag_real, hidden, d_out, d_dec),
        loss,
    )
    g_out[...] = dot_nt(hidden[...], d_out[...])

    width = quant.shape[0]
    for part, shift in enumerate((before, lambda values: values, after)):
        g_dec[part * width : (part + 1) * width, :] = dot_nt(shift(quant[...]), d_dec[...])
    latent_back(clip_count, dec, d_dec, mask, slope, hidden)

    samples = sig.shape[0]
    for part, shift in enumerate((before, lambda values: values, after)):
        g_enc[part * samples : (part + 1) * samples, :] = dot_nt(shift(sig[...]), hidden[...])
    swap = pltpu.make_async_remote_copy(
        src_ref=loss, dst_ref=met, send_sem=send_sem, recv_sem=recv_sem,
        device_id=(spot, 1 - side), device_id_type=pl.DeviceIdType.MESH,
    )
    swap.start()
    swap.wait()
    loss_out[...] = loss[...] + met[...]


def local_call(audio_t, lengths, codes, disc, score, enc, dec, out, books):
    clip_count, samples, _ = audio_t.shape
    width = disc.shape[1]
    total = clip_count * LANES
    table = spectral_table(samples)
    vmem = pl.BlockSpec(memory_space=pltpu.VMEM)
    smem = pl.BlockSpec(memory_space=pltpu.SMEM)
    return pl.pallas_call(
        local_kernel,
        out_shape=(
            jax.ShapeDtypeStruct((3 * samples, width), F32),
            jax.ShapeDtypeStruct((3 * width, width), F32),
            jax.ShapeDtypeStruct((width, samples), F32),
            jax.ShapeDtypeStruct((4, CB, width // 2), F32),
            jax.ShapeDtypeStruct((1, WIDE), F32),
        ),
        in_specs=[vmem, smem] + [vmem] * 9,
        out_specs=[vmem] * 5,
        scratch_shapes=[
            pltpu.VMEM((samples, LANES), BF),
            pltpu.VMEM((8, LANES), jnp.int32),
            pltpu.VMEM((8, total), jnp.int32),
            pltpu.VMEM((1, total), F32),
            pltpu.VMEM((samples, total), BF),
            pltpu.VMEM((width, 3 * samples), BF),
            pltpu.VMEM((width, 128), F32),
            pltpu.VMEM((width, total), BF),
            pltpu.VMEM((samples // 2, total), F32),
            pltpu.VMEM((2, width // 2, 2 * CB), BF),
            pltpu.VMEM((width, total), BF),
            pltpu.VMEM((width, total), BF),
            pltpu.VMEM((width, 3 * samples), BF),
            pltpu.VMEM((width, total), BF),
            pltpu.VMEM((width, 3 * width), BF),
            pltpu.VMEM((samples, width), BF),
            pltpu.VMEM((samples, total), BF),
            pltpu.VMEM((width, total), BF),
            pltpu.VMEM((1, WIDE), F32),
            pltpu.VMEM((1, WIDE), F32),
            pltpu.SemaphoreType.DMA,
            pltpu.SemaphoreType.DMA,
        ],
        compiler_params=pltpu.CompilerParams(
            vmem_limit_bytes=56 << 20, collective_id=0, has_side_effects=True
        ),
        name="train_local",
    )(
        audio_t, lengths, codes, disc, score.reshape(1, width),
        jnp.asarray(table, BF), jnp.asarray(table.T, BF), enc, dec, out, books,
    )


def shards(
    audio, lengths, codes, disc_weight, disc_score, params, params_mom, params_avg, books,
    books_mom, books_avg,
):
    clip_count, slot_count, samples = audio.shape
    width = disc_weight.shape[1]
    half_width = width // 2
    side = lax.axis_index("grp")
    shared = lax.all_gather(params.astype(BF), "dp", axis=0, tiled=True)
    table = lax.all_gather(books.astype(BF), ("grp", "dp"), axis=1, tiled=True)
    enc_size = 3 * samples * width
    dec_size = 3 * width * width
    enc_weight = shared[:enc_size].reshape(3 * samples, width)
    dec_weight = shared[enc_size : enc_size + dec_size].reshape(3 * width, width)
    out_weight = shared[enc_size + dec_size :].reshape(width, samples)
    codebook = table.reshape(2, 2 * CB, half_width)
    local_count = jnp.sum(
        lax.dynamic_slice_in_dim(lengths, side * clip_count, clip_count, 0)
    ).astype(F32)
    frame_count = lax.psum(local_count, ("dp", "grp"))
    grad_enc, grad_dec, grad_out, grad_book, lost = local_call(
        jnp.swapaxes(audio, 1, 2), lengths, codes, disc_weight, disc_score,
        enc_weight, dec_weight, out_weight, codebook,
    )
    grad_shared = jnp.concatenate(
        [grad_enc.reshape(-1), grad_dec.reshape(-1), grad_out.reshape(-1)]
    )
    grad_shared = lax.psum(grad_shared.astype(BF), "grp").astype(F32)
    grad_book = lax.psum_scatter(
        grad_book.reshape(2, -1), "grp", scatter_dimension=0, tiled=True
    )
    shared_part = lax.psum_scatter(grad_shared, "dp", scatter_dimension=0, tiled=True)
    book_part = lax.psum_scatter(grad_book, "dp", scatter_dimension=1, tiled=True)
    loss_sum = lax.psum(jnp.sum(lost), "dp")
    all_clips = clip_count * lax.axis_size("dp") * lax.axis_size("grp")
    root = math.sqrt(131.0 * all_clips)
    shard_length = params.shape[0]
    spots = lax.axis_index("dp") * shard_length + jnp.arange(shard_length)
    rate = (
        jnp.where(spots < enc_size, 0.65, jnp.where(spots < enc_size + dec_size, 0.14, 0.2)) * root
    )
    shared_grad = shared_part / frame_count
    mom_new = MOMENTUM * params_mom + shared_grad
    param_new = params - rate * (shared_grad + MOMENTUM * mom_new)
    avg_new = AVERAGE * params_avg + (1.0 - AVERAGE) * param_new
    book_rate = 3.9 * math.sqrt(131.0 * all_clips * CB)
    book_grad_mean = book_part / frame_count
    book_mom_new = MOMENTUM * books_mom + book_grad_mean
    book_new = books - book_rate * (book_grad_mean + MOMENTUM * book_mom_new)
    book_avg_new = AVERAGE * books_avg + (1.0 - AVERAGE) * book_new
    return (
        param_new, mom_new, avg_new, book_new, book_mom_new, book_avg_new, loss_sum, frame_count,
    )


def solution(mesh):
    in_specs = (
        P(("dp", "grp"), None, None), P("dp"), P(None, None, "dp", None), P(), P(), P("dp"),
        P("dp"), P("dp"), P("grp", "dp"), P("grp", "dp"), P("grp", "dp"),
    )
    out_specs = (
        P("dp"), P("dp"), P("dp"), P("grp", "dp"), P("grp", "dp"), P("grp", "dp"), P(), P(),
    )
    return jax.shard_map(shards, mesh=mesh, in_specs=in_specs, out_specs=out_specs, check_vma=False)
```

time: 775 us -> 714 us (0.921)
  matrix products: 112 us -> 0 us
  Pallas kernels: 0 us -> 85.2 us
  local copies, waits for them, and re-layouts: 84.2 us -> 25.2 us
  blocking collectives: 322 us -> 286 us
  waiting for transfers between devices: 176 us -> 210 us
  other arithmetic: 52.2 us -> 82 us
    dot_general x18 -> x0, matrix products: 112 us -> none  [the longest x9 51.7 us: project(): jnp.einsum('bsk,kd->bsd', operand, weights, preferred_element_type=jnp.fl...]
    pallas_call x0 -> x1, Pallas kernels: none -> 85.2 us  [local_call(): pl.pallas_call(local_kernel, out_shape=(jax.ShapeDtypeStruct((3 * samples...]
    unnamed x5 -> x7, waiting for transfers between devices: 65.4 us -> 123 us
    all_gather x0 -> x1, other arithmetic: none -> 44.5 us  [shards(): table = lax.all_gather(books.astype(BF), ('grp', 'dp'), axis=1, tiled=True)]
    all_to_all x4 -> x0, blocking collectives: 37.2 us -> none  [the longest x1 11.8 us: shards(): lax.all_to_all(d_joined, 'grp', split_axis=2, concat_axis=0, tiled=True)]
    convert_element_type x4 -> x0, local copies, waits for them, and re-layouts: 32 us -> none  [the longest x1 8.29 us: shards(): d_quant.astype(jnp.float32) * pair_three + commit_slope]
    slice x6 -> x0, local copies, waits for them, and re-layouts: 31.2 us -> none  [the longest x2 12.6 us: unstack_three(): before[:, 1:]]
    psum x1, waiting for transfers between devices: 21.4 us -> 0.01 us  [shards(): grad_shared = lax.psum(grad_shared.astype(BF), 'grp').astype(F32)]
  transfers between devices with their start and end apart: 4 -> 5, of which waited for: 4 -> 3; matrix products, arithmetic and copies ran while one was open for 7% -> 9% of each run, Pallas kernels for 0% -> 0%
where the time goes in v1:
time: 714 us; the launch traced here: 704 us
  blocking collectives  286 us (40%)
  waiting for transfers between devices  210 us (29%)
  Pallas kernels  85.2 us (12%)
  other arithmetic  82 us (11%)
  local copies, waits for them, and re-layouts  25.2 us (4%)
  between operations  16.1 us (2%)
    unnamed x1, blocking collectives  246 us
    unnamed x7, waiting for transfers between devices  123 us
    pallas_call x1, Pallas kernels, local_call(): pl.pallas_call(local_kernel, out_shape=(jax.ShapeDtypeStruct((3 * samples...  85.2 us
    all_gather x1, waiting for transfers between devices, shards(): table = lax.all_gather(books.astype(BF), ('grp', 'dp'), axis=1, tiled=True)  65.6 us
    all_gather x1, other arithmetic, shards(): table = lax.all_gather(books.astype(BF), ('grp', 'dp'), axis=1, tiled=True)  44.5 us
    psum x1, blocking collectives, shards(): frame_count = lax.psum(local_count, ('dp', 'grp'))  40 us
    concatenate x1, other arithmetic, shards(): jnp.concatenate([grad_enc.reshape(-1), grad_dec.reshape(-1), grad_out.res...  24.5 us
    all_gather x1, waiting for transfers between devices, shards(): shared = lax.all_gather(params.astype(BF), 'dp', axis=0, tiled=True)  21.1 us
  transfers between devices with their start and end apart: 5, of which 3 were waited for; matrix products, arithmetic and copies ran while one was open for 9% of the time, Pallas kernels for 0%

profile of v1, /device:TPU:0, one launch (start us, length us, event | category | flops | bytes accessed | tf_op | source)
XLA Modules:
  0.0 703.9 jit_solution(17033571623946042585)
XLA Ops:
  7.2 1.7 convert_element_type.14
  8.9 1.7 convert_element_type.13
  10.6 0.0 all-reduce.9.cloned.1.call-start
  10.7 65.6 %all-gather.5.cloned.1.call-done = bf16[1,1048576]{1,0:T(2,128)(2,1)} async-done(((bf16[1,32768]{1,0:T(2,128)(2,1)}), bf16[1,1048576]{1,0:T(2,128)(2,1)}) %all-gather.5.cloned.1.call-update) | async-done | bytes 2097168 | tf_op jit(solution)/shard_map/all_gather | solution.py:346
  76.3 44.5 %reduce = bf16[1048576]{0:T(1024)(128)(2,1)S(1)} reduce(bf16[1,1048576]{1,0:T(2,128)(2,1)} %all-gather.5.cloned.1.call-done, bf16[]{:T(256)} %constant.65), dimensions={0}, to_apply=%all_gather.7.reduce_sub_computation | reduce | bytes 4194306 | tf_op jit(solution)/shard_map/all_gather | solution.py:346
  120.9 2.2 reshape.60.books
  123.0 21.1 %all-gather.3.cloned.1.call-done = bf16[1441792]{0:T(1024)(128)(2,1)} async-done(((bf16[90112]{0:T(1024)(128)(2,1)}), bf16[1441792]{0:T(1024)(128)(2,1)}) %all-gather.3.cloned.1.call-update) | async-done | bytes 2883600 | tf_op jit(solution)/shard_map/all_gather | solution.py:345
  144.1 1.4 slice-done
  145.6 2.2 slice.32.dec
  147.8 1.6 slice.30.enc
  149.4 1.1 reshape.59.out
  150.5 85.2 %train_local.1 = (f32[960,512]{1,0:T(8,128)}, f32[1536,512]{1,0:T(8,128)}, f32[512,320]{1,0:T(8,128)}, f32[4,1024,256]{2,1,0:T(8,128)}, f32[1,512]{1,0:T(1,128)}) custom-call(bf16[12,320,232]{2,1,0:T(8,128)(2,1)} %bitcast.14, s32[24]{0:T(128)} %lens.1, s32[2,2,24,232]{3,2,1,0:T(8,128)} %codes.1, bf16[960,512]{1,0:T(8,128)(2,1)} %disc.1, f32[1,512]{1,0:T(1,128)} %bitcast.15, ...), custom_call_target="tpu_custom_call" | custom-call | tf_op jit(solution)/shard_map/train_local/pallas_call | solution.py:292
  235.7 2.4 convert_bitcast_fusion
  238.1 0.8 copy.24
  238.9 0.2 convert_bitcast_fusion.1
  239.1 0.4 copy.23
  239.5 0.5 copy-done.2
  240.1 0.5 reshape.63
  240.6 24.5 %pad_maximum_fusion = bf16[1441792]{0:T(1024)(128)(2,1)} fusion(bf16[163840]{0:T(1024)(128)(2,1)S(1)} %reshape.63, bf16[786432]{0:T(1024)(128)(2,1)S(1)} %bitcast.12, bf16[491520]{0:T(1024)(128)(2,1)S(1)} %bitcast.13), kind=kLoop, calls=%fused_computation | loop fusion | flops 8650752 | bytes 5767168 | tf_op jit(solution)/shard_map/concatenate | solution.py:361
  265.1 0.0 all-reduce.11.cloned.1.call-start
  265.1 7.0 reshape.64
  272.2 0.6 copy-done.9
  272.8 0.7 dynamic-slice_reduce_fusion
  274.1 40.0 %psum.22 = f32[]{:T(128)} all-reduce(f32[]{:T(128)S(6)} %convert_element_type.16), channel_id=1, replica_groups=mesh['dp'=16,'grp'=2] {'dp','grp'}, use_global_device_ids=true, to_apply=%region_3.0 | all-reduce | flops 1 | bytes 8 | tf_op jit(solution)/shard_map/psum | solution.py:356
  314.1 0.6 dynamic-slice
  314.7 0.6 dynamic-slice.2
  316.6 0.6 reduce_sum.19
  317.2 245.5 %all-reduce.14 = (f32[1441792]{0:T(1024)}, f32[]{:T(128)}) all-reduce(bf16[1441792]{0:T(1024)(128)(2,1)} %all-reduce.9.cloned.1.call-done, f32[]{:T(128)} %reduce_sum.19), channel_id=2, replica_groups=mesh['dp'=16,'grp'=2] {'dp'}, use_global_device_ids=true, to_apply=%region_1.0.clone | all-reduce | flops 1441793 | bytes 8650760
  562.8 5.8 constant_dynamic-slice_fusion
  568.6 2.9 multiply_add_fusion
  571.5 122.9 %all-reduce.13.cloned.1.call-done = f32[1,524288]{1,0:T(1,128)} async-done(((f32[1,524288]{1,0:T(1,128)}), f32[1,524288]{1,0:T(1,128)}) %all-reduce.13.cloned.1.call-update) | async-done | bytes 2097168
  694.4 2.8 multiply_add_fusion.2
  (38 shorter events, 0.3 us)
Async XLA Ops:
  7.2 69.2 %all-gather.5.cloned.1.call-start = ((), (), s32[]{:S(2)}) async-start(), calls=%async_computation.1 | async-start | bytes 4325376 | tf_op jit(solution)/shard_map/all_gather | solution.py:346
  8.9 135.3 %all-gather.3.cloned.1.call-start = ((), (), s32[]{:S(2)}) async-start(), calls=%async_computation | async-start | bytes 3063808 | tf_op jit(solution)/shard_map/all_gather | solution.py:345
  10.6 306.6 %all-reduce.9.cloned.1.call-start = ((), (), s32[]{:S(2)}) async-start(), calls=%async_computation.2 | async-start | bytes 5767168 | tf_op jit(solution)/shard_map/psum | solution.py:364
  144.1 1.4 slice-start
  145.6 2.2 slice-start.1
  147.8 1.6 slice-start.2
  235.7 3.2 copy-start
  238.9 1.1 copy-start.2
  265.1 297.7 %all-reduce.11.cloned.1.call-start = ((), (), s32[]{:S(2)}) async-start(), calls=%async_computation.3 | async-start | bytes 8388608
  272.1 0.7 copy-start.9
  272.1 42.0 %copy-start.11 = (u32[32]{0:T(128)S(1)}, u32[32]{0:T(128)}, u32[]{:S(2)}) copy-start(u32[32]{0:T(128)} %constant.55) | copy-start | bytes 388
  272.1 42.6 %copy-start.10 = (u32[32]{0:T(128)S(1)}, u32[32]{0:T(128)}, u32[]{:S(2)}) copy-start(u32[32]{0:T(128)} %constant.59) | copy-start | bytes 388
  272.1 44.5 %copy-start.8 = (f32[1,512]{1,0:T(1,128)S(1)}, f32[1,512]{1,0:T(1,128)}, u32[]{:S(2)}) copy-start(f32[1,512]{1,0:T(1,128)} %get-tuple-element.17) | copy-start | bytes 6148
  272.1 422.2 %all-reduce.13.cloned.1.call-start = ((), (), s32[]{:S(2)}) async-start(), calls=%async_computation.4 | async-start | bytes 4194304
  562.8 5.8 copy-start.1
  562.8 5.8 copy-start.4
  562.8 5.8 copy-start.5
  568.5 125.8 %copy-start.3 = (f32[1,32768]{1,0:T(1,128)S(1)}, f32[1,32768]{1,0:T(1,128)}, u32[]{:S(2)}) copy-start(f32[1,32768]{1,0:T(1,128)} %param.21) | copy-start | bytes 393220
  568.5 125.8 %copy-start.6 = (f32[1,32768]{1,0:T(1,128)S(1)}, f32[1,32768]{1,0:T(1,128)}, u32[]{:S(2)}) copy-start(f32[1,32768]{1,0:T(1,128)} %param.23) | copy-start | bytes 393220
  568.5 125.8 %copy-start.7 = (f32[1,32768]{1,0:T(1,128)S(1)}, f32[1,32768]{1,0:T(1,128)}, u32[]{:S(2)}) copy-start(f32[1,32768]{1,0:T(1,128)} %param.22) | copy-start | bytes 393220
Sparse Core Ops, SparseCore 0:
  11.6 64.7 all-gather.4
  79.7 64.4 all-gather.2
  265.2 21.7 all-reduce.8
  289.5 29.6 all-reduce.10
  568.7 125.6 all-reduce.12
